TPU v7x, 512 devices: a whole 4x4x16 slice. The times are simulated.
512 devices in a mesh: sec: 4 (over y), tile: 128 (over x, z, core).
Axes of the slice: x: 4, y: 4, z: 16, core: 2. Of those that a mesh axis runs over, the one named last changes fastest.
Arguments:
- atm_flux: bfloat16 [20, 4194304], P(None, ('sec', 'tile')), may hold values from -6 to 6
- remap_rank: int32 [65536], P(('sec', 'tile')), may hold values from 0 to 127, as said below
- pair_src: int32 [98304], P('tile'), may hold values from 0 to 511, as said below
- pair_dst: int32 [98304], P('tile'), may hold values from 0 to 63, as said below
- pair_count: int32 [128], P('tile'), may hold values from 512 to 768, as said below
- pair_weight: bfloat16 [98304, 4096], P('tile'), may hold values from 0 to 1.5, as said below
- ocean_state: float32 [20, 524288], P('sec', 'tile'), may hold values from -6 to 6
- exchange_coef: float32 [20], P('sec'), may hold values from 0.2 to 1
- ocean_mask: int32 [524288], P('tile'), may hold values 0 or 1
Outputs:
- merged_flux: float32 [20, 524288], P('sec', 'tile')
Inputs may be any that keep to these rules, and one draw needn't show every extreme that they name: `remap_rank`: among each device's 128 consecutive blocks, every tile index occurs exactly once. `pair_src`: the first 512 slots of each tile index name every assigned block once. `pair_dst`: the first 64 slots of each tile index name every destination block once. `pair_count`: some tile index has all 768 slots live. `pair_weight`: entries are nonnegative; each diagonal entry is at least 0.5.
All inputs are finite; a program needn't handle non-finite values. No bound on the sum of `ocean_mask` on one device may be relied on, other than what follows from the above.
Results may differ from a plain program's by a relative error of at most 0.0003.
Values may be sent and summed in bfloat16 or wider, within the bound.
A program may use at most 64 MiB of HBM per device.

v0:
```python
import jax
import jax.numpy as jnp
from jax import lax
from jax.sharding import PartitionSpec as P

BLK = 64


def from_root(value, axis, root):
    mine = lax.axis_index(axis) == root
    return lax.psum(jnp.where(mine, value, jnp.zeros_like(value)), axis)


def pair_terms(sources, slot_src, slot_dst, weights, live_pairs, dst_blocks):
    count_pairs = slot_src.shape[0]
    width = sources.shape[2]
    squares = weights.reshape(count_pairs, width, width)
    gathered = jnp.take(sources, slot_src, axis=1)
    contrib = jnp.einsum("fpi,pji->fpj", gathered, squares, preferred_element_type=jnp.float32)
    contrib = contrib * live_pairs[None, :, None]
    row_totals = jnp.sum(squares, axis=2, dtype=jnp.float32) * live_pairs[:, None]
    stacked = jnp.concatenate([contrib, row_totals[None, :, :]], axis=0)
    selector = (slot_dst[:, None] == jnp.arange(dst_blocks)[None, :]).astype(jnp.float32)
    combined = jnp.einsum("fpj,pb->fbj", stacked, selector, precision=lax.Precision.HIGHEST)
    return (combined[:-1], combined[-1])


def per_device(
    atm_flux,
    remap_rank,
    pair_src,
    pair_dst,
    pair_count,
    pair_weight,
    ocean_state,
    exchange_coef,
    ocean_mask,
):
    n_tile = lax.axis_size("tile")
    fields, columns = atm_flux.shape
    src_blocks = columns // BLK
    per_peer = src_blocks // n_tile
    ranking = jnp.argsort(remap_rank, stable=True)
    blocks = atm_flux.reshape(fields, src_blocks, BLK)
    ranked = jnp.take(blocks, ranking, axis=1).reshape(fields, 1, n_tile, per_peer * BLK)
    moved = lax.all_to_all(ranked, "tile", split_axis=2, concat_axis=2, tiled=True)
    received = lax.all_to_all(moved, "sec", split_axis=0, concat_axis=1, tiled=True)
    group_fields = received.shape[0]
    sources = received.reshape(group_fields, -1, BLK)
    dst_blocks = ocean_mask.shape[0] // BLK
    slot_total = pair_src.shape[0]
    count = pair_count[0]
    live_pairs = (jnp.arange(slot_total) < count).astype(jnp.float32)
    summed, weight_rows = pair_terms(
        sources, pair_src, pair_dst, pair_weight, live_pairs, dst_blocks
    )
    remapped = (summed / weight_rows[None, :, :]).reshape(group_fields, dst_blocks * BLK)
    local_speed = jnp.sqrt(remapped[0] * remapped[0] + remapped[1] * remapped[1] + 0.25)
    wind_speed = from_root(local_speed, "sec", 0)
    oceanic = ocean_mask.astype(jnp.float32)
    return remapped + oceanic[None, :] * exchange_coef[:, None] * wind_speed[None, :] * (
        ocean_state - remapped
    )


def solution(mesh):
    in_specs = (
        P(None, ("sec", "tile")),
        P(("sec", "tile")),
        P("tile"),
        P("tile"),
        P("tile"),
        P("tile", None),
        P("sec", "tile"),
        P("sec"),
        P("tile"),
    )
    out_specs = P("sec", "tile")
    return jax.shard_map(
        per_device, mesh=mesh, in_specs=in_specs, out_specs=out_specs, check_vma=False
    )
```

profile of v0, /device:TPU:4, one launch (start us, length us, event | category | flops | bytes accessed | tf_op | source)
XLA Modules:
  0.0 114.6 jit_solution(943203665232585984)
XLA Ops:
  0.0 3.2 %sort.17 = (s32[128]{0:T(128)}, s32[128]{0:T(128)S(1)}) sort(s32[128]{0:T(128)} %param.10, s32[128]{0:T(128)S(1)} %iota.15), dimensions={0}, to_apply=%region_0.0 | sort | flops 896 | bytes 2048 | tf_op jit(solution)/shard_map/jit(argsort)/sort | solution.py:43
  3.2 1.7 %reshape.81 = bf16[20,128,64]{2,1,0:T(8,128)(2,1)S(1)} reshape(bf16[20,8192]{1,0:T(8,128)(2,1)} %param.9) | data formatting | bytes 655360 | tf_op jit(solution)/shard_map/reshape | solution.py:44
  4.9 0.4 copy.21
  5.3 0.8 gather_fusion
  6.1 0.2 fusion.22
  6.3 1.1 reshape.107
  7.4 19.7 %all-to-all-start = ((bf16[128,2,640]{2,1,0:T(2,128)(2,1)}), bf16[128,2,640]{2,1,0:T(2,128)(2,1)S(1)}, u32[]{:S(2)}, u32[]{:S(2)}) async-start(bf16[128,2,640]{2,1,0:T(2,128)(2,1)} %reshape.107), calls=%async_computation | async-start | bytes 655360 | tf_op jit(solution)/shard_map/all_to_all | solution.py:46
  27.1 0.0 copy-start.2
  27.2 8.7 %copy.26 = bf16[768,4096]{0,1:T(8,128)(2,1)} copy(bf16[768,4096]{1,0:T(8,128)(2,1)} %param.14) | data formatting | bytes 12582912 | tf_op args[5]
  36.5 0.0 copy-done.2
  36.5 4.5 %convert_reduce_fusion = f32[768,64]{0,1:T(8,128)S(1)} fusion(bf16[768,4096]{0,1:T(8,128)(2,1)} %copy.26), kind=kLoop, calls=%fused_computation.2 | loop fusion | flops 6242304 | bytes 6488064 | tf_op jit(solution)/shard_map/reduce_sum | solution.py:21
  41.0 11.4 %all-to-all-done = bf16[128,2,640]{2,1,0:T(2,128)(2,1)S(1)} async-done(((bf16[128,2,640]{2,1,0:T(2,128)(2,1)}), bf16[128,2,640]{2,1,0:T(2,128)(2,1)S(1)}, u32[]{:S(2)}, u32[]{:S(2)}) %all-to-all-start) | async-done | bytes 327712 | tf_op jit(solution)/shard_map/all_to_all | solution.py:46
  52.4 0.6 reshape.108
  53.0 1.2 %copy.23 = bf16[20,1,128,64]{2,3,1,0:T(8,128)(2,1)} copy(bf16[20,1,128,64]{3,0,1,2:T(8,128)(2,1)S(1)} %bitcast.40) | data formatting | bytes 655360 | tf_op jit(solution)/shard_map/all_to_all | solution.py:46
  54.2 4.5 %all-to-all-start.1 = ((bf16[20,1,128,64]{2,3,1,0:T(8,128)(2,1)}), bf16[20,1,128,64]{2,3,1,0:T(8,128)(2,1)S(1)}, u32[]{:S(2)}, u32[]{:S(2)}) async-start(bf16[20,1,128,64]{2,3,1,0:T(8,128)(2,1)} %copy.23), calls=%async_computation.1 | async-start | bytes 655360 | tf_op jit(solution)/shard_map/all_to_all | solution.py:47
  58.7 0.0 copy-start.1
  58.7 18.4 %copy.27 = bf16[768,64,64]{2,1,0:T(8,128)(2,1)} copy(bf16[768,64,64]{0,2,1:T(8,128)(2,1)} %bitcast.38) | data formatting | bytes 12582912 | tf_op jit(solution)/shard_map/reshape | solution.py:17
  77.1 0.0 copy-done.1
  77.1 0.0 all-to-all-done.1
  77.1 0.5 copy.29
  77.7 3.2 %gather_fusion.1 = bf16[768,5,64]{2,1,0:T(8,128)(2,1)} fusion(bf16[5,512,64]{2,0,1:T(8,128)(2,1)S(1)} %bitcast.39, s32[1024]{0:T(1024)S(1)} %pad_clamp_fusion), kind=kCustom, calls=%fused_computation.1 | custom fusion | bytes 986112 | tf_op jit(solution)/shard_map/jit(_take)/gather | solution.py:18
  80.9 11.4 %multiply_bitcast_fusion = f32[5,768,64]{2,0,1:T(8,128)S(1)} fusion(bf16[768,64,64]{2,1,0:T(8,128)(2,1)} %copy.27, bf16[768,5,64]{2,1,0:T(8,128)(2,1)} %gather_fusion.1, f32[768]{0:T(1024)S(1)} %get-tuple-element.7, pred[768]{0:T(1024)(128)(4,1)S(1)} %get-tuple-element.8), kind=kOutput, calls=%fused_computation.3 | convolution fusion | flops 31948800 | bytes 7769856 | tf_op jit(solution)/shard_map/fpi,pji->fpj/dot_general | solution.py:19
  92.3 0.0 copy-start.3
  92.3 0.0 copy-start
  92.3 0.0 copy-start.4
  92.3 1.7 %copy.28 = f32[5,768,64]{1,2,0:T(8,128)} copy(f32[5,768,64]{2,0,1:T(8,128)S(1)} %multiply_bitcast_fusion) | data formatting | bytes 1966080 | tf_op jit(solution)/shard_map/mul | solution.py:20
  94.0 0.0 copy-done.3
  94.0 2.2 %fusion.7 = f32[6,64,64]{2,1,0:T(8,128)S(1)} fusion(f32[1,768,64]{1,2,0:T(8,128)S(1)} %bitcast_multiply_fusion, f32[5,768,64]{1,2,0:T(8,128)} %copy.28, s32[768]{0:T(1024)S(1)} %copy-done.3), kind=kOutput, calls=%fused_computation.11 | convolution fusion | flops 226836480 | bytes 1281024 | tf_op jit(solution)/shard_map/fpj,pb->fbj/dot_general | solution.py:24
  96.3 0.1 reshape.84
  96.4 0.1 reshape.87
  96.5 17.4 %psum.7 = f32[4096]{0:T(1024)S(1)} all-reduce(f32[4096]{0:T(1024)S(1)} %reshape.87), channel_id=1, replica_groups=mesh['sec'=4,'tile'=128] {'sec'}, use_global_device_ids=true, to_apply=%region_2.3 | all-reduce | flops 4096 | bytes 32768 | tf_op jit(solution)/shard_map/psum | solution.py:11
  113.8 0.0 copy-done
  113.8 0.0 copy-done.4
  113.8 0.7 multiply_add_fusion
  (12 shorter events, 0.1 us)
Async XLA Ops:
  7.4 45.0 %all-to-all-start = ((bf16[128,2,640]{2,1,0:T(2,128)(2,1)}), bf16[128,2,640]{2,1,0:T(2,128)(2,1)S(1)}, u32[]{:S(2)}, u32[]{:S(2)}) async-start(bf16[128,2,640]{2,1,0:T(2,128)(2,1)} %reshape.107), calls=%async_computation | async-start | bytes 655360 | tf_op jit(solution)/shard_map/all_to_all | solution.py:46
  27.1 9.4 %copy-start.2 = (s32[768]{0:T(1024)S(1)}, s32[768]{0:T(1024)}, u32[]{:S(2)}) copy-start(s32[768]{0:T(1024)} %param.11) | copy-start | bytes 9220
  54.2 22.9 %all-to-all-start.1 = ((bf16[20,1,128,64]{2,3,1,0:T(8,128)(2,1)}), bf16[20,1,128,64]{2,3,1,0:T(8,128)(2,1)S(1)}, u32[]{:S(2)}, u32[]{:S(2)}) async-start(bf16[20,1,128,64]{2,3,1,0:T(8,128)(2,1)} %copy.23), calls=%async_computation.1 | async-start | bytes 655360 | tf_op jit(solution)/shard_map/all_to_all | solution.py:47
  58.7 18.4 %copy-start.1 = (s32[4096]{0:T(1024)S(1)}, s32[4096]{0:T(1024)}, u32[]{:S(2)}) copy-start(s32[4096]{0:T(1024)} %param.17) | copy-start | bytes 49156
  92.3 1.7 %copy-start.3 = (s32[768]{0:T(1024)S(1)}, s32[768]{0:T(1024)}, u32[]{:S(2)}) copy-start(s32[768]{0:T(1024)} %param.12) | copy-start | bytes 9220
  92.3 21.5 %copy-start = (f32[5,4096]{1,0:T(8,128)S(1)}, f32[5,4096]{1,0:T(8,128)}, u32[]{:S(2)}) copy-start(f32[5,4096]{1,0:T(8,128)} %param.15) | copy-start | bytes 245764
  92.3 21.5 %copy-start.4 = (f32[5]{0:T(128)S(1)}, f32[5]{0:T(128)}, u32[]{:S(2)}) copy-start(f32[5]{0:T(128)} %param.16) | copy-start | bytes 64
where the time goes:
time: 116 us; the launch traced here: 115 us
  local copies, waits for them, and re-layouts  38.5 us (33%)
  starting transfers between devices  24.2 us (21%)
  blocking collectives  17.4 us (15%)
  matrix products  13.6 us (12%)
  waiting for transfers between devices  11.4 us (10%)
  other arithmetic  8.72 us (8%)
    all_to_all x1, starting transfers between devices, per_device(): lax.all_to_all(ranked, 'tile', split_axis=2, concat_axis=2, tiled=True)  19.7 us
    reshape x1, local copies, waits for them, and re-layouts, pair_terms(): squares = weights.reshape(count_pairs, width, width)  18.4 us
    psum x1, blocking collectives, from_root(): return lax.psum(jnp.where(mine, value, jnp.zeros_like(value)), axis)  17.4 us
    dot_general x1, matrix products, pair_terms(): jnp.einsum('fpi,pji->fpj', gathered, squares, preferred_element_type=jnp....  11.4 us
    all_to_all x1, waiting for transfers between devices, per_device(): lax.all_to_all(ranked, 'tile', split_axis=2, concat_axis=2, tiled=True)  11.4 us
    unnamed x13, local copies, waits for them, and re-layouts  10.5 us
    reduce_sum x1, other arithmetic, pair_terms(): jnp.sum(squares, axis=2, dtype=jnp.float32) * live_pairs[:, None]  4.49 us
    all_to_all x1, starting transfers between devices, per_device(): lax.all_to_all(moved, 'sec', split_axis=0, concat_axis=1, tiled=True)  4.46 us
  transfers between devices with their start and end apart: 2, of which 1 were waited for; matrix products, arithmetic and copies ran while one was open for 28% of the time, Pallas kernels for 0%

commit v1 on v0

v1 whole, which is shorter than its diff:
```python
import functools

import jax
import jax.numpy as jnp
from jax import lax
from jax.experimental import pallas as pl
from jax.experimental.pallas import tpu as pltpu
from jax.sharding import PartitionSpec as P

MESH = pl.DeviceIdType.MESH
F32, BF16, I32 = jnp.float32, jnp.bfloat16, jnp.int32
PAIRS, SOURCES, CELLS = 768, 512, 4096

OFFSETS = [8, 7, -7, 0, 6, -6, 5, -5, 4, -4, 3, -3, 2, -2, 1, -1]
PLACE = {dz: j for j, dz in enumerate(OFFSETS)}
CHUNKS = 4
SPAN = {0: (0, 1), 8: (15, 1)}
for _d in range(1, 8):
    SPAN[_d] = (2 * _d - 1, 2)


def iota(shape, dim):
    return lax.broadcasted_iota(I32, shape, dim)


def dot(a, b):
    return jnp.dot(a, b, preferred_element_type=F32)


def onehot(cond):
    return jnp.where(cond, 1.0, 0.0).astype(BF16)


def split(value):
    high = value.astype(BF16)
    return high, (value - high.astype(F32)).astype(BF16)


def kernel(
    x_ref, rank_ref, src_ref, dst_ref, count_ref, w_hbm, ocean_ref, coef_ref, mask_ref,
    out_ref,
    inv_v, inv_s, xpad, blocks, xsend, xrecv, units, zrecv, ysend, yrecv, wraw, wtile,
    field_rows, pack_rows, swap_rows, group_rows, dup_rows, keep, fill, select, expand,
    terms, sums, spread, final,
    inv_sem, w_sem, x_ss, x_rs, z_ss, z_rs, y_ss, y_rs,
):
    sec = lax.axis_index("sec")
    me = lax.axis_index("tile")
    x, z, c = me >> 5, (me >> 1) & 15, me & 1

    def tile_of(xx, zz, cc):
        return xx * 32 + zz * 2 + cc

    def peer(i):
        return tile_of(x ^ (i >> 1), z, c ^ (i & 1))

    def along(dz):
        return tile_of(x, (z + dz) & 15, c)

    barrier = pltpu.get_barrier_semaphore()
    for dz in OFFSETS:
        if dz:
            pl.semaphore_signal(
                barrier, inc=1, device_id={"tile": along(dz)}, device_id_type=MESH
            )
    for i in range(1, 8):
        pl.semaphore_signal(barrier, inc=1, device_id={"tile": peer(i)}, device_id_type=MESH)
    for i in range(1, 4):
        pl.semaphore_signal(barrier, inc=1, device_id={"sec": sec ^ i}, device_id_type=MESH)

    lane8 = iota((8, 128), 1)
    inv = jnp.zeros((8, 128), I32)
    for a in range(128):
        inv = jnp.where(lane8 == rank_ref[a], a, inv)
    inv_v[...] = inv
    inv_copy = pltpu.make_async_copy(inv_v, inv_s, inv_sem)
    inv_copy.start()

    w_copies = [
        pltpu.make_async_copy(
            w_hbm.at[pl.ds(128 * i, 128)], wraw.at[pl.ds(128 * i, 128)], w_sem.at[i]
        )
        for i in range(6)
    ]
    for copy in w_copies:
        copy.start()

    row, col = iota((32, 32), 0), iota((32, 32), 1)
    r, h = row & 15, row >> 4
    pair_field = 5 * (r >> 1) + 2 * (r & 1) + h
    last_field = 4 + 10 * (r - 8) + 5 * h
    wanted = jnp.where(r < 8, pair_field, last_field)
    field_rows[...] = onehot((col == wanted) & (r < 10))
    xpad[16:32, :] = jnp.zeros((16, 8192), BF16)
    xpad[0:16, :] = x_ref[0:16, :]
    xpad[16:20, :] = x_ref[16:20, :]

    low16 = iota((16, 128), 1) < 64

    def build(i, _):
        at = pl.multiple_of(i * 512, 512)
        packed = dot(field_rows[...], xpad[:, pl.ds(at, 512)])
        for q in range(4):
            a = packed[0:16, 128 * q : 128 * q + 128]
            b = packed[16:32, 128 * q : 128 * q + 128]
            blocks[i * 8 + 2 * q] = jnp.where(low16, a, pltpu.roll(b, 64, 1)).astype(BF16)
            blocks[i * 8 + 2 * q + 1] = jnp.where(low16, pltpu.roll(a, 64, 1), b).astype(BF16)
        return 0

    lax.fori_loop(0, 16, build, 0)

    row, col = iota((80, 128), 0), iota((80, 128), 1)
    pack_rows[...] = onehot(col == (row & 7) * 16 + (row >> 3))

    inv_copy.wait()
    x_copies = {}
    for chunk in range(CHUNKS):
        for i in range(8):
            for j in range(4 * chunk, 4 * chunk + 4):
                target = tile_of(x ^ (i >> 1), (z + OFFSETS[j]) & 15, c ^ (i & 1))
                block = blocks[inv_s[0, target]]
                if i == 0:
                    xrecv[0, j] = block
                else:
                    xsend[i, j] = block
        if chunk == 0:
            pl.semaphore_wait(barrier, 25)
        for i in (6, 7, 4, 5, 2, 3, 1):
            part = pl.ds(4 * chunk, 4)
            x_copies[i, chunk] = pltpu.make_async_remote_copy(
                xsend.at[i, part], xrecv.at[i, part], x_ss.at[i, chunk], x_rs.at[i, chunk],
                device_id={"tile": peer(i)}, device_id_type=MESH,
            )
            x_copies[i, chunk].start()

    row, col = iota((256, 256), 0), iota((256, 256), 1)
    swap_rows[...] = onehot(((row & 15) == (col >> 4)) & ((row >> 4) == (col & 15)))
    row, col = iota((128, 80), 0), iota((128, 80), 1)
    g, i8, r4 = sec ^ (row >> 5), (row >> 2) & 7, row & 3
    picked = jnp.where(r4 == 0, 0, jnp.where(r4 == 3, 8 + (g >> 1), 2 * g + r4 - 1))
    group_rows[...] = onehot(col == picked * 8 + i8)
    row, col = iota((128, 64), 0), iota((128, 64), 1)
    q = (row >> 2) & 3
    from_rolled = jnp.where((q == 1) | (q == 2), 32, 0)
    dup_rows[...] = onehot(col == from_rolled + (row >> 4) * 4 + (row & 3))
    row, col = iota((128, 256), 0), iota((128, 256), 1)
    inside = (((col & 127) < 64) == ((row & 15) < 8))
    unit_row = jnp.where((sec & 1) == 1, 3, 7)
    ones_here = inside & ((row & 7) == unit_row)
    keep[...] = jnp.where(inside & ((row & 7) != unit_row), 1.0, 0.0).astype(F32)
    fill[...] = jnp.where(ones_here, 1.0, 0.0).astype(F32)

    def compact(chunk):
        for i in range(1, 8):
            x_copies[i, chunk].wait_recv()
        for j in (4 * chunk, 4 * chunk + 2):
            both = jnp.concatenate(
                [xrecv[:, j].reshape(128, 128), xrecv[:, j + 1].reshape(128, 128)], axis=1
            )
            packed = dot(pack_rows[...], both).astype(BF16)
            units[j] = packed[:, :128]
            units[j + 1] = packed[:, 128:]

    z_copies = {}

    def send(j):
        dz = OFFSETS[j]
        if dz:
            z_copies[dz] = pltpu.make_async_remote_copy(
                units.at[j], zrecv.at[j], z_ss.at[j], z_rs.at[j],
                device_id={"tile": along(dz)}, device_id_type=MESH,
            )
            z_copies[dz].start()

    y_copies = {}

    def forward(d):
        at, n = SPAN[d]
        if d == 0:
            arrived = units[PLACE[0]]
        elif d == 8:
            z_copies[8].wait_recv()
            arrived = zrecv[PLACE[8]]
        else:
            z_copies[d].wait_recv()
            z_copies[-d].wait_recv()
            arrived = jnp.concatenate([zrecv[PLACE[d]], zrecv[PLACE[-d]]], axis=1)
        grouped = dot(group_rows[...], arrived).astype(BF16)
        for i in range(4):
            for u in range(n):
                piece = grouped[32 * i : 32 * i + 32, 128 * u : 128 * u + 128]
                if i == 0:
                    yrecv[0, at + u] = piece
                else:
                    ysend[i, at + u] = piece
        for i in (2, 1, 3):
            part = pl.ds(at, n)
            y_copies[i, d] = pltpu.make_async_remote_copy(
                ysend.at[i, part], yrecv.at[i, part], y_ss.at[i, d], y_rs.at[i, d],
                device_id={"sec": sec ^ i}, device_id_type=MESH,
            )
            y_copies[i, d].start()

    def place_sources(d, which):
        at, n = SPAN[d]
        for i in which:
            if i:
                y_copies[i, d].wait_recv()
            parts = []
            for u in range(n):
                plain = yrecv[i, at + u]
                rolled = pltpu.roll(plain.astype(F32), 64, 1).astype(BF16)
                parts.append(jnp.concatenate([plain, rolled], axis=0))
            both = parts[0] if n == 1 else jnp.concatenate(parts, axis=1)
            width = 128 * n
            made = dot(dup_rows[...], both) * keep[:, :width] + fill[:, :width]
            made = made.astype(BF16)
            for u in range(n):
                origin = (z + 16 - d) & 15 if u == 0 else (z + d) & 15
                for o in range(8):
                    slot = (sec ^ i) * 128 + tile_of(x ^ (o >> 1), origin, c ^ (o & 1))
                    sources_at(slot)[...] = made[16 * o : 16 * o + 16, 128 * u : 128 * u + 128]

    def sources_at(slot):
        return spread.at[slot]

    def weight_group(k, _):
        at = pl.multiple_of(k * 16, 16)
        pieces = [
            jnp.concatenate(
                [
                    wraw[pl.ds(at, 16), 128 * m : 128 * m + 128],
                    wraw[pl.ds(at, 16), 128 * (m + 16) : 128 * (m + 16) + 128],
                ],
                axis=1,
            )
            for m in range(16)
        ]
        made = dot(swap_rows[...], jnp.concatenate(pieces, axis=0)).astype(BF16)
        wtile[pl.ds(at, 16), 0:16, :] = made[:, :128].reshape(16, 16, 128)
        wtile[pl.ds(at, 16), 16:32, :] = made[:, 128:].reshape(16, 16, 128)
        return 0

    def weights(first, last):
        for i in range(6):
            if first <= 8 * i < last:
                w_copies[i].wait()
        lax.fori_loop(first, last, weight_group, 0)

    def selectors():
        row = iota((64, PAIRS), 0)
        dst = jnp.broadcast_to(dst_ref[...].reshape(1, PAIRS), (64, PAIRS))
        block = 2 * (row & 31) + (row >> 5)
        live = iota((64, PAIRS), 1) < count_ref[0]
        chosen = onehot((dst == block) & live)
        for g4 in range(4):
            row, col = iota((PAIRS, 384), 0), iota((PAIRS, 384), 1)
            n = col - jnp.where(col >= 192, 192, 0)
            thin = onehot(row == 4 * n + g4)
            select[64 * g4 : 64 * g4 + 64, :] = dot(chosen, thin).astype(BF16)
        row, col = iota((512, 128), 0), iota((512, 128), 1)
        j = 2 * (row & 31) + ((row >> 7) & 1)
        expand[...] = onehot(col == (row >> 8) * 64 + j)

    for chunk in range(CHUNKS):
        compact(chunk)
        for j in range(4 * chunk, 4 * chunk + 4):
            send(j)
    order = [0, 8, 7, 6, 5, 4, 3, 2, 1]
    done = 0
    selectors()
    for n, d in enumerate(order):
        forward(d)
        upto = min(48, done + 6)
        weights(done, upto)
        done = upto
        if n >= 2:
            place_sources(order[n - 2], (0, 1, 2, 3))
    for copy in x_copies.values():
        copy.wait_send()
    for copy in z_copies.values():
        copy.wait_send()
    for d in order[-2:]:
        place_sources(d, (0, 1, 2, 3))
    for copy in y_copies.values():
        copy.wait_send()

    lane = iota((16, 128), 1)

    def pair_tile(t, _):
        for s in range(4):
            k = (t * 4 + s) * 8
            left = jnp.concatenate([spread[src_ref[k + o]] for o in range(8)], axis=0)
            right = wtile[pl.ds(k, 8)].reshape(256, 128)
            made = lax.dot_general(
                left, right, (((1,), (1,)), ((), ())), preferred_element_type=F32
            )
            for q in range(2):
                part = [
                    made[64 * q + 16 * o : 64 * q + 16 * o + 16, 128 * q : 128 * q + 128]
                    for o in range(4)
                ]
                value = jnp.where(
                    lane < 64,
                    jnp.where(lane < 32, part[0], part[1]),
                    jnp.where(lane < 96, part[2], part[3]),
                )
                at = pl.multiple_of((2 * (t * 4 + s) + q) * 16, 16)
                terms[pl.ds(at, 16), :] = value
        return 0

    lax.fori_loop(0, 24, pair_tile, 0)

    lane = iota((64, 128), 1)
    odd = (sec & 1) == 1
    spot = {0: 5, 1: 0, 2: 2, 3: jnp.where(odd, 7, 4), 4: 6, 5: 1, 6: 3, 7: jnp.where(odd, 4, 7)}
    for r in range(0, 16, 2):
        sides = []
        for k in (r, r + 1):
            high, low = split(terms[pl.ds(k, 192, stride=16), :])
            sides.append(jnp.concatenate([high, low], axis=0))
        made = dot(select[...], jnp.concatenate(sides, axis=1))
        for o in range(2):
            part = [made[64 * g : 64 * g + 64, 128 * o : 128 * o + 128] for g in range(4)]
            value = jnp.where(
                lane < 64,
                jnp.where(lane < 32, part[0], part[1]),
                jnp.where(lane < 96, part[2], part[3]),
            )
            high, low = split(value)
            p, idx = (r + o) >> 3, (r + o) & 7
            at = spot[idx] * 32
            if not isinstance(at, int):
                at = pl.multiple_of(at, 32)
            for parity in range(2):
                lanes = pl.ds((parity * 2 + p) * 128, 128)
                sums[0, pl.ds(at, 32), lanes] = high[32 * parity : 32 * parity + 32]
                sums[1, pl.ds(at, 32), lanes] = low[32 * parity : 32 * parity + 32]
    final[...] = dot(sums[0], expand[...]) + dot(sums[1], expand[...])

    row8 = iota((8, 128), 0)
    coef = jnp.zeros((8, 128), F32)
    for f in range(5):
        coef = jnp.where(row8 == f, coef_ref[f], coef)
    coef = coef[0:5]
    wind = (row8 == 5) | (row8 == 6)
    oceanic = mask_ref[...].reshape(1, CELLS).astype(F32)
    for b in range(32):
        lanes = pl.ds(128 * b, 128)
        v = final[pl.ds(b, 8, stride=32), :]
        weight = jnp.broadcast_to(v[7:8], (8, 128))
        remapped = v / weight
        squares = jnp.where(wind, remapped * remapped, 0.0)
        speed = jnp.sqrt(jnp.sum(squares, axis=0, keepdims=True) + 0.25)
        own = remapped[0:5]
        factor = coef * (oceanic[:, 128 * b : 128 * b + 128] * speed)
        out_ref[:, lanes] = own + factor * (ocean_ref[:, lanes] - own)


def per_device(*args):
    vmem = pl.BlockSpec(memory_space=pltpu.VMEM)
    smem = pl.BlockSpec(memory_space=pltpu.SMEM)
    hbm = pl.BlockSpec(memory_space=pl.ANY)
    dma = pltpu.SemaphoreType.DMA
    return pl.pallas_call(
        kernel,
        out_shape=jax.ShapeDtypeStruct((5, CELLS), F32),
        in_specs=[vmem, smem, smem, vmem, smem, hbm, vmem, smem, vmem],
        out_specs=vmem,
        scratch_shapes=[
            pltpu.VMEM((8, 128), I32),
            pltpu.SMEM((8, 128), I32),
            pltpu.VMEM((32, 8192), BF16),
            pltpu.VMEM((128, 16, 128), BF16),
            pltpu.VMEM((8, 16, 16, 128), BF16),
            pltpu.VMEM((8, 16, 16, 128), BF16),
            pltpu.VMEM((16, 80, 128), BF16),
            pltpu.VMEM((16, 80, 128), BF16),
            pltpu.VMEM((4, 16, 32, 128), BF16),
            pltpu.VMEM((4, 16, 32, 128), BF16),
            pltpu.VMEM((PAIRS, 4096), BF16),
            pltpu.VMEM((PAIRS, 32, 128), BF16),
            pltpu.VMEM((32, 32), BF16),
            pltpu.VMEM((80, 128), BF16),
            pltpu.VMEM((256, 256), BF16),
            pltpu.VMEM((128, 80), BF16),
            pltpu.VMEM((128, 64), BF16),
            pltpu.VMEM((128, 256), F32),
            pltpu.VMEM((128, 256), F32),
            pltpu.VMEM((256, 384), BF16),
            pltpu.VMEM((512, 128), BF16),
            pltpu.VMEM((192 * 16, 128), F32),
            pltpu.VMEM((2, 256, 512), BF16),
            pltpu.VMEM((SOURCES, 16, 128), BF16),
            pltpu.VMEM((256, 128), F32),
            dma(()),
            dma((6,)),
            dma((8, CHUNKS)),
            dma((8, CHUNKS)),
            dma((16,)),
            dma((16,)),
            dma((4, 9)),
            dma((4, 9)),
        ],
        compiler_params=pltpu.CompilerParams(
            collective_id=0, has_side_effects=True, vmem_limit_bytes=48 * 2**20
        ),
    )(*args)


def solution(mesh):
    in_specs = (
        P(None, ("sec", "tile")),
        P(("sec", "tile")),
        P("tile"),
        P("tile"),
        P("tile"),
        P("tile", None),
        P("sec", "tile"),
        P("sec"),
        P("tile"),
    )
    return jax.shard_map(
        per_device, mesh=mesh, in_specs=in_specs, out_specs=P("sec", "tile"), check_vma=False
    )
```

time: 116 us -> 65.2 us (0.56)
  the two profiles are of different devices: /device:TPU:4 before, /device:TPU:1 now
where the time goes in v1:
time: 65.2 us; the launch traced here: 64.9 us
  Pallas kernels  58.3 us (89%)
  local copies, waits for them, and re-layouts  5.95 us (9%)
  between operations  0.67 us (1%)
    pallas_call x1, Pallas kernels, per_device(): pl.pallas_call(kernel, out_shape=jax.ShapeDtypeStruct((5, CELLS), F32), i...  58.3 us
    unnamed x15, local copies, waits for them, and re-layouts  5.95 us

profile of v1, /device:TPU:1, one launch (start us, length us, event | category | flops | bytes accessed | tf_op | source)
XLA Modules:
  0.0 64.9 jit_solution(15882204327839820579)
XLA Ops:
  0.7 0.0 copy-start
  0.7 1.0 %copy-done = bf16[20,8192]{1,0:T(8,128)(2,1)S(1)} copy-done((bf16[20,8192]{1,0:T(8,128)(2,1)S(1)}, bf16[20,8192]{1,0:T(8,128)(2,1)}, u32[]{:S(2)}) %copy-start) | copy-done | bytes 327704
  1.6 0.0 copy-start.1
  1.7 0.9 %copy-done.1 = f32[5,4096]{1,0:T(8,128)S(1)} copy-done((f32[5,4096]{1,0:T(8,128)S(1)}, f32[5,4096]{1,0:T(8,128)}, u32[]{:S(2)}) %copy-start.1) | copy-done | bytes 81944
  2.6 0.0 copy-start.2
  2.6 0.7 %copy-done.2 = s32[4096]{0:T(1024)S(1)} copy-done((s32[4096]{0:T(1024)S(1)}, s32[4096]{0:T(1024)}, u32[]{:S(2)}) %copy-start.2) | copy-done | bytes 16408
  3.3 0.0 copy-start.3
  3.3 0.7 %copy-done.3 = s32[768]{0:T(1024)S(1)} copy-done((s32[768]{0:T(1024)S(1)}, s32[768]{0:T(1024)}, u32[]{:S(2)}) %copy-start.3) | copy-done | bytes 3096
  4.0 0.0 copy-start.4
  4.0 0.7 %copy-done.4 = s32[768]{0:T(1024)S(1)} copy-done((s32[768]{0:T(1024)S(1)}, s32[768]{0:T(1024)}, u32[]{:S(2)}) %copy-start.4) | copy-done | bytes 3096
  4.6 0.0 copy-start.5
  4.6 0.7 %copy-done.5 = s32[128]{0:T(128)S(1)} copy-done((s32[128]{0:T(128)S(1)}, s32[128]{0:T(128)}, u32[]{:S(2)}) %copy-start.5) | copy-done | bytes 536
  5.3 0.0 copy-start.6
  5.3 0.7 %copy-done.6 = f32[5]{0:T(128)S(1)} copy-done((f32[5]{0:T(128)S(1)}, f32[5]{0:T(128)}, u32[]{:S(2)}) %copy-start.6) | copy-done | bytes 44
  6.0 58.3 %shard_map.91 = f32[5,4096]{1,0:T(8,128)S(1)} custom-call(bf16[20,8192]{1,0:T(8,128)(2,1)S(1)} %copy-done, s32[128]{0:T(128)S(1)} %copy-done.5, s32[768]{0:T(1024)S(1)} %copy-done.3, s32[768]{0:T(1024)S(1)} %copy-done.4, s32[1]{0:T(128)S(6)} %copy.11.count_ref, bf16[768,4096]{1,0:T(8,128)(2,1)} %w_hbm.1, f32[5,4096]{1,0:T(8,128)S(1)} %copy-done.1, ...), custom_call_target="tpu_custom_call" | custom-call | tf_op jit(solution)/shard_map/pallas_call | solution.py:365
  64.3 0.7 %copy.12 = f32[5,4096]{1,0:T(8,128)} copy(f32[5,4096]{1,0:T(8,128)S(1)} %shard_map.91) | data formatting | bytes 163840
Async XLA Ops:
  0.7 1.0 %copy-start = (bf16[20,8192]{1,0:T(8,128)(2,1)S(1)}, bf16[20,8192]{1,0:T(8,128)(2,1)}, u32[]{:S(2)}) copy-start(bf16[20,8192]{1,0:T(8,128)(2,1)} %x_ref.1) | copy-start | bytes 983044
  1.6 0.9 %copy-start.1 = (f32[5,4096]{1,0:T(8,128)S(1)}, f32[5,4096]{1,0:T(8,128)}, u32[]{:S(2)}) copy-start(f32[5,4096]{1,0:T(8,128)} %ocean_ref.1) | copy-start | bytes 245764
  2.6 0.7 %copy-start.2 = (s32[4096]{0:T(1024)S(1)}, s32[4096]{0:T(1024)}, u32[]{:S(2)}) copy-start(s32[4096]{0:T(1024)} %mask_ref.1) | copy-start | bytes 49156
  3.3 0.7 %copy-start.3 = (s32[768]{0:T(1024)S(1)}, s32[768]{0:T(1024)}, u32[]{:S(2)}) copy-start(s32[768]{0:T(1024)} %src_ref.1) | copy-start | bytes 9220
  4.0 0.7 %copy-start.4 = (s32[768]{0:T(1024)S(1)}, s32[768]{0:T(1024)}, u32[]{:S(2)}) copy-start(s32[768]{0:T(1024)} %dst_ref.1) | copy-start | bytes 9220
  4.6 0.7 %copy-start.5 = (s32[128]{0:T(128)S(1)}, s32[128]{0:T(128)}, u32[]{:S(2)}) copy-start(s32[128]{0:T(128)} %rank_ref.1) | copy-start | bytes 1540
  5.3 0.7 %copy-start.6 = (f32[5]{0:T(128)S(1)}, f32[5]{0:T(128)}, u32[]{:S(2)}) copy-start(f32[5]{0:T(128)} %coef_ref.1) | copy-start | bytes 64

commit v2 on v1

--- a/solution.py
+++ b/solution.py
@@ -11,9 +11,12 @@
 F32, BF16, I32 = jnp.float32, jnp.bfloat16, jnp.int32
 PAIRS, SOURCES, CELLS = 768, 512, 4096
 
-OFFSETS = [8, 7, -7, 0, 6, -6, 5, -5, 4, -4, 3, -3, 2, -2, 1, -1]
+OFFSETS = [8, 1, -1, 0, 7, -7, 2, -2, 6, -6, 3, -3, 5, -5, 4, -4]
 PLACE = {dz: j for j, dz in enumerate(OFFSETS)}
-CHUNKS = 4
+BOUNDS = [0, 4, 8, 12, 16]
+CHUNKS = len(BOUNDS) - 1
+FIRST, SECOND, EACH = 8, 28, 5
+UNROLL = 16
 SPAN = {0: (0, 1), 8: (15, 1)}
 for _d in range(1, 8):
     SPAN[_d] = (2 * _d - 1, 2)
@@ -37,12 +40,13 @@
 
 
 def kernel(
-    x_ref, rank_ref, src_ref, dst_ref, count_ref, w_hbm, ocean_ref, coef_ref, mask_ref,
+    x_hbm, rank_hbm, src_hbm, dst_hbm, count_hbm, w_hbm, ocean_hbm, coef_hbm, mask_hbm,
     out_ref,
+    x_ref, rank_ref, src_ref, dst_ref, count_ref, ocean_ref, coef_ref, mask_ref, in_sem,
     inv_v, inv_s, xpad, blocks, xsend, xrecv, units, zrecv, ysend, yrecv, wraw, wtile,
     field_rows, pack_rows, swap_rows, group_rows, dup_rows, keep, fill, select, expand,
     terms, sums, spread, final,
-    inv_sem, w_sem, x_ss, x_rs, z_ss, z_rs, y_ss, y_rs,
+    inv_sem, w_sem, x_ss, x_rs, z_ss, z_rs, y_ss, y_rs, known,
 ):
     sec = lax.axis_index("sec")
     me = lax.axis_index("tile")
@@ -58,16 +62,27 @@
         return tile_of(x, (z + dz) & 15, c)
 
     barrier = pltpu.get_barrier_semaphore()
-    for dz in OFFSETS:
-        if dz:
-            pl.semaphore_signal(
-                barrier, inc=1, device_id={"tile": along(dz)}, device_id_type=MESH
-            )
+    for dz in (2, -2, 1, -1):
+        pl.semaphore_signal(barrier, inc=1, device_id={"tile": along(dz)}, device_id_type=MESH)
     for i in range(1, 8):
         pl.semaphore_signal(barrier, inc=1, device_id={"tile": peer(i)}, device_id_type=MESH)
     for i in range(1, 4):
         pl.semaphore_signal(barrier, inc=1, device_id={"sec": sec ^ i}, device_id_type=MESH)
 
+    ins = [
+        pltpu.make_async_copy(source, target, in_sem.at[i])
+        for i, (source, target) in enumerate(
+            [
+                (rank_hbm, rank_ref), (x_hbm, x_ref), (src_hbm, src_ref), (dst_hbm, dst_ref),
+                (count_hbm, count_ref), (coef_hbm, coef_ref), (mask_hbm, mask_ref),
+                (ocean_hbm, ocean_ref),
+            ]
+        )
+    ]
+    for copy in ins:
+        copy.start()
+
+    ins[0].wait()
     lane8 = iota((8, 128), 1)
     inv = jnp.zeros((8, 128), I32)
     for a in range(128):
@@ -92,8 +107,22 @@
     wanted = jnp.where(r < 8, pair_field, last_field)
     field_rows[...] = onehot((col == wanted) & (r < 10))
     xpad[16:32, :] = jnp.zeros((16, 8192), BF16)
+    ins[1].wait()
     xpad[0:16, :] = x_ref[0:16, :]
     xpad[16:20, :] = x_ref[16:20, :]
+
+    def tell(reach, which):
+        for way, dz in enumerate((reach, -reach)):
+            pl.semaphore_signal(
+                known.at[which, way], inc=1, device_id={"tile": along(dz)}, device_id_type=MESH
+            )
+
+    def hear(which):
+        for way in range(2):
+            pl.semaphore_wait(known.at[which, way], 1)
+
+    pl.semaphore_wait(barrier, 14)
+    tell(2, 0)
 
     low16 = iota((16, 128), 1) < 64
 
@@ -109,51 +138,21 @@
 
     lax.fori_loop(0, 16, build, 0)
 
-    row, col = iota((80, 128), 0), iota((80, 128), 1)
-    pack_rows[...] = onehot(col == (row & 7) * 16 + (row >> 3))
-
-    inv_copy.wait()
     x_copies = {}
-    for chunk in range(CHUNKS):
-        for i in range(8):
-            for j in range(4 * chunk, 4 * chunk + 4):
-                target = tile_of(x ^ (i >> 1), (z + OFFSETS[j]) & 15, c ^ (i & 1))
-                block = blocks[inv_s[0, target]]
-                if i == 0:
-                    xrecv[0, j] = block
-                else:
-                    xsend[i, j] = block
-        if chunk == 0:
-            pl.semaphore_wait(barrier, 25)
+
+    def exchange(chunk):
+        part = pl.ds(BOUNDS[chunk], BOUNDS[chunk + 1] - BOUNDS[chunk])
         for i in (6, 7, 4, 5, 2, 3, 1):
-            part = pl.ds(4 * chunk, 4)
             x_copies[i, chunk] = pltpu.make_async_remote_copy(
                 xsend.at[i, part], xrecv.at[i, part], x_ss.at[i, chunk], x_rs.at[i, chunk],
                 device_id={"tile": peer(i)}, device_id_type=MESH,
             )
             x_copies[i, chunk].start()
 
-    row, col = iota((256, 256), 0), iota((256, 256), 1)
-    swap_rows[...] = onehot(((row & 15) == (col >> 4)) & ((row >> 4) == (col & 15)))
-    row, col = iota((128, 80), 0), iota((128, 80), 1)
-    g, i8, r4 = sec ^ (row >> 5), (row >> 2) & 7, row & 3
-    picked = jnp.where(r4 == 0, 0, jnp.where(r4 == 3, 8 + (g >> 1), 2 * g + r4 - 1))
-    group_rows[...] = onehot(col == picked * 8 + i8)
-    row, col = iota((128, 64), 0), iota((128, 64), 1)
-    q = (row >> 2) & 3
-    from_rolled = jnp.where((q == 1) | (q == 2), 32, 0)
-    dup_rows[...] = onehot(col == from_rolled + (row >> 4) * 4 + (row & 3))
-    row, col = iota((128, 256), 0), iota((128, 256), 1)
-    inside = (((col & 127) < 64) == ((row & 15) < 8))
-    unit_row = jnp.where((sec & 1) == 1, 3, 7)
-    ones_here = inside & ((row & 7) == unit_row)
-    keep[...] = jnp.where(inside & ((row & 7) != unit_row), 1.0, 0.0).astype(F32)
-    fill[...] = jnp.where(ones_here, 1.0, 0.0).astype(F32)
-
     def compact(chunk):
         for i in range(1, 8):
             x_copies[i, chunk].wait_recv()
-        for j in (4 * chunk, 4 * chunk + 2):
+        for j in range(BOUNDS[chunk], BOUNDS[chunk + 1], 2):
             both = jnp.concatenate(
                 [xrecv[:, j].reshape(128, 128), xrecv[:, j + 1].reshape(128, 128)], axis=1
             )
@@ -242,12 +241,16 @@
         return 0
 
     def weights(first, last):
+        if first == last:
+            return
         for i in range(6):
             if first <= 8 * i < last:
                 w_copies[i].wait()
         lax.fori_loop(first, last, weight_group, 0)
 
     def selectors():
+        for copy in ins[2:]:
+            copy.wait()
         row = iota((64, PAIRS), 0)
         dst = jnp.broadcast_to(dst_ref[...].reshape(1, PAIRS), (64, PAIRS))
         block = 2 * (row & 31) + (row >> 5)
@@ -262,18 +265,58 @@
         j = 2 * (row & 31) + ((row >> 7) & 1)
         expand[...] = onehot(col == (row >> 8) * 64 + j)
 
+    inv_copy.wait()
+    for i in range(8):
+        for j in range(16):
+            target = tile_of(x ^ (i >> 1), (z + OFFSETS[j]) & 15, c ^ (i & 1))
+            block = blocks[inv_s[0, target]]
+            if i == 0:
+                xrecv[0, j] = block
+            else:
+                xsend[i, j] = block
+    hear(0)
+    tell(4, 1)
+    for chunk in range(CHUNKS):
+        exchange(chunk)
+
+    row, col = iota((80, 128), 0), iota((80, 128), 1)
+    pack_rows[...] = onehot(col == (row & 7) * 16 + (row >> 3))
+
+
+    row, col = iota((256, 256), 0), iota((256, 256), 1)
+    swap_rows[...] = onehot(((row & 15) == (col >> 4)) & ((row >> 4) == (col & 15)))
+    row, col = iota((128, 80), 0), iota((128, 80), 1)
+    g, i8, r4 = sec ^ (row >> 5), (row >> 2) & 7, row & 3
+    picked = jnp.where(r4 == 0, 0, jnp.where(r4 == 3, 8 + (g >> 1), 2 * g + r4 - 1))
+    group_rows[...] = onehot(col == picked * 8 + i8)
+    row, col = iota((128, 64), 0), iota((128, 64), 1)
+    q = (row >> 2) & 3
+    from_rolled = jnp.where((q == 1) | (q == 2), 32, 0)
+    dup_rows[...] = onehot(col == from_rolled + (row >> 4) * 4 + (row & 3))
+    row, col = iota((128, 256), 0), iota((128, 256), 1)
+    inside = (((col & 127) < 64) == ((row & 15) < 8))
+    unit_row = jnp.where((sec & 1) == 1, 3, 7)
+    ones_here = inside & ((row & 7) == unit_row)
+    keep[...] = jnp.where(inside & ((row & 7) != unit_row), 1.0, 0.0).astype(F32)
+    fill[...] = jnp.where(ones_here, 1.0, 0.0).astype(F32)
+
+    weights(0, FIRST)
+    hear(1)
     for chunk in range(CHUNKS):
         compact(chunk)
-        for j in range(4 * chunk, 4 * chunk + 4):
+        for j in range(BOUNDS[chunk], BOUNDS[chunk + 1]):
             send(j)
-    order = [0, 8, 7, 6, 5, 4, 3, 2, 1]
-    done = 0
+    order = [0, 1, 8, 2, 7, 3, 6, 4, 5]
+    forward(0)
+    weights(FIRST, SECOND)
     selectors()
+    done = SECOND
     for n, d in enumerate(order):
-        forward(d)
-        upto = min(48, done + 6)
-        weights(done, upto)
-        done = upto
+        if n:
+            forward(d)
+            upto = min(48, done + EACH)
+            weights(done, upto)
+            done = upto
         if n >= 2:
             place_sources(order[n - 2], (0, 1, 2, 3))
     for copy in x_copies.values():
@@ -288,8 +331,8 @@
     lane = iota((16, 128), 1)
 
     def pair_tile(t, _):
-        for s in range(4):
-            k = (t * 4 + s) * 8
+        for s in range(UNROLL):
+            k = (t * UNROLL + s) * 8
             left = jnp.concatenate([spread[src_ref[k + o]] for o in range(8)], axis=0)
             right = wtile[pl.ds(k, 8)].reshape(256, 128)
             made = lax.dot_general(
@@ -305,11 +348,11 @@
                     jnp.where(lane < 32, part[0], part[1]),
                     jnp.where(lane < 96, part[2], part[3]),
                 )
-                at = pl.multiple_of((2 * (t * 4 + s) + q) * 16, 16)
+                at = pl.multiple_of((2 * (t * UNROLL + s) + q) * 16, 16)
                 terms[pl.ds(at, 16), :] = value
         return 0
 
-    lax.fori_loop(0, 24, pair_tile, 0)
+    lax.fori_loop(0, 96 // UNROLL, pair_tile, 0)
 
     lane = iota((64, 128), 1)
     odd = (sec & 1) == 1
@@ -359,15 +402,23 @@
 
 def per_device(*args):
     vmem = pl.BlockSpec(memory_space=pltpu.VMEM)
-    smem = pl.BlockSpec(memory_space=pltpu.SMEM)
-    hbm = pl.BlockSpec(memory_space=pl.ANY)
+    hbm = pl.BlockSpec(memory_space=pltpu.HBM)
     dma = pltpu.SemaphoreType.DMA
     return pl.pallas_call(
         kernel,
         out_shape=jax.ShapeDtypeStruct((5, CELLS), F32),
-        in_specs=[vmem, smem, smem, vmem, smem, hbm, vmem, smem, vmem],
+        in_specs=[hbm] * 9,
         out_specs=vmem,
         scratch_shapes=[
+            pltpu.VMEM((20, 8192), BF16),
+            pltpu.SMEM((128,), I32),
+            pltpu.SMEM((PAIRS,), I32),
+            pltpu.VMEM((PAIRS,), I32),
+            pltpu.SMEM((1,), I32),
+            pltpu.VMEM((5, CELLS), F32),
+            pltpu.SMEM((5,), F32),
+            pltpu.VMEM((CELLS,), I32),
+            dma((8,)),
             pltpu.VMEM((8, 128), I32),
             pltpu.SMEM((8, 128), I32),
             pltpu.VMEM((32, 8192), BF16),
@@ -401,9 +452,10 @@
             dma((16,)),
             dma((4, 9)),
             dma((4, 9)),
+            pltpu.SemaphoreType.REGULAR((2, 2)),
         ],
         compiler_params=pltpu.CompilerParams(
-            collective_id=0, has_side_effects=True, vmem_limit_bytes=48 * 2**20
+            collective_id=0, has_side_effects=True, vmem_limit_bytes=56 * 2**20
         ),
     )(*args)
 

time: 65.2 us -> 53.7 us (0.82)
  Pallas kernels: 58.3 us -> 51.3 us
  local copies, waits for them, and re-layouts: 5.95 us -> 1.57 us
    pallas_call x1, Pallas kernels: 58.3 us -> 51.3 us  [per_device(): pl.pallas_call(kernel, out_shape=jax.ShapeDtypeStruct((5, CELLS), F32), i...]
    unnamed x15 -> x1, local copies, waits for them, and re-layouts: 5.95 us -> 1.57 us
where the time goes in v2:
time: 53.7 us; the launch traced here: 53.6 us
  Pallas kernels  51.3 us (96%)
  local copies, waits for them, and re-layouts  1.57 us (3%)
  between operations  0.66 us (1%)
    pallas_call x1, Pallas kernels, per_device(): pl.pallas_call(kernel, out_shape=jax.ShapeDtypeStruct((5, CELLS), F32), i...  51.3 us
    unnamed x1, local copies, waits for them, and re-layouts  1.57 us

profile of v2, /device:TPU:1, one launch (start us, length us, event | category | flops | bytes accessed | tf_op | source)
XLA Modules:
  0.0 53.6 jit_solution(17595935787996182602)
XLA Ops:
  0.7 51.3 %shard_map.91 = f32[5,4096]{1,0:T(8,128)} custom-call(bf16[20,8192]{1,0:T(8,128)(2,1)} %x_hbm.1, s32[128]{0:T(128)} %rank_hbm.1, s32[768]{0:T(1024)} %src_hbm.1, s32[768]{0:T(1024)} %dst_hbm.1, s32[1]{0:T(128)S(6)} %copy.11.count_hbm, bf16[768,4096]{1,0:T(8,128)(2,1)} %w_hbm.1, f32[5,4096]{1,0:T(8,128)} %ocean_hbm.1, f32[5]{0:T(128)} %coef_hbm.1, s32[4096]{0:T(1024)} %mask_hbm.1), custom_call_target="tpu_custom_call" | custom-call | tf_op jit(solution)/shard_map/pallas_call | solution.py:407
  52.0 1.6 %copy.12 = f32[5,4096]{1,0:T(8,128)} copy(f32[5,4096]{1,0:T(8,128)} %shard_map.91) | data formatting | bytes 163840

commit v3 on v2

--- a/solution.py
+++ b/solution.py
@@ -13,10 +13,10 @@
 
 OFFSETS = [8, 1, -1, 0, 7, -7, 2, -2, 6, -6, 3, -3, 5, -5, 4, -4]
 PLACE = {dz: j for j, dz in enumerate(OFFSETS)}
-BOUNDS = [0, 4, 8, 12, 16]
+BOUNDS = [0, 4, 10, 16]
 CHUNKS = len(BOUNDS) - 1
 FIRST, SECOND, EACH = 8, 28, 5
-UNROLL = 16
+UNROLL = 32
 SPAN = {0: (0, 1), 8: (15, 1)}
 for _d in range(1, 8):
     SPAN[_d] = (2 * _d - 1, 2)

time: 53.7 us -> 52.7 us (0.981)
  Pallas kernels: 51.3 us -> 50.3 us
    pallas_call x1, Pallas kernels: 51.3 us -> 50.3 us  [per_device(): pl.pallas_call(kernel, out_shape=jax.ShapeDtypeStruct((5, CELLS), F32), i...]
where the time goes in v3:
time: 52.7 us; the launch traced here: 52.5 us
  Pallas kernels  50.3 us (95%)
  local copies, waits for them, and re-layouts  1.57 us (3%)
  between operations  0.66 us (1%)
    pallas_call x1, Pallas kernels, per_device(): pl.pallas_call(kernel, out_shape=jax.ShapeDtypeStruct((5, CELLS), F32), i...  50.3 us
    unnamed x1, local copies, waits for them, and re-layouts  1.57 us

profile of v3, /device:TPU:1, one launch (start us, length us, event | category | flops | bytes accessed | tf_op | source)
XLA Modules:
  0.0 52.5 jit_solution(17457721242005100387)
XLA Ops:
  0.7 50.3 %shard_map.91 = f32[5,4096]{1,0:T(8,128)} custom-call(bf16[20,8192]{1,0:T(8,128)(2,1)} %x_hbm.1, s32[128]{0:T(128)} %rank_hbm.1, s32[768]{0:T(1024)} %src_hbm.1, s32[768]{0:T(1024)} %dst_hbm.1, s32[1]{0:T(128)S(6)} %copy.11.count_hbm, bf16[768,4096]{1,0:T(8,128)(2,1)} %w_hbm.1, f32[5,4096]{1,0:T(8,128)} %ocean_hbm.1, f32[5]{0:T(128)} %coef_hbm.1, s32[4096]{0:T(1024)} %mask_hbm.1), custom_call_target="tpu_custom_call" | custom-call | tf_op jit(solution)/shard_map/pallas_call | solution.py:407
  50.9 1.6 %copy.12 = f32[5,4096]{1,0:T(8,128)} copy(f32[5,4096]{1,0:T(8,128)} %shard_map.91) | data formatting | bytes 163840

commit v4 on v3

--- a/solution.py
+++ b/solution.py
@@ -324,9 +324,11 @@
     for copy in z_copies.values():
         copy.wait_send()
     for d in order[-2:]:
-        place_sources(d, (0, 1, 2, 3))
+        place_sources(d, (0,))
     for copy in y_copies.values():
         copy.wait_send()
+    for d in order[-2:]:
+        place_sources(d, (1, 3, 2))
 
     lane = iota((16, 128), 1)
 

time: 52.7 us -> 52.9 us (level)
  no operation moved by 1% of the time
where the time goes in v4:
time: 52.9 us; the launch traced here: 52.5 us
  Pallas kernels  50.3 us (95%)
  local copies, waits for them, and re-layouts  1.57 us (3%)
  between operations  0.66 us (1%)
    pallas_call x1, Pallas kernels, per_device(): pl.pallas_call(kernel, out_shape=jax.ShapeDtypeStruct((5, CELLS), F32), i...  50.3 us
    unnamed x1, local copies, waits for them, and re-layouts  1.57 us

profile of v4, /device:TPU:1, one launch (start us, length us, event | category | flops | bytes accessed | tf_op | source)
XLA Modules:
  0.0 52.5 jit_solution(2945241675985952190)
XLA Ops:
  0.7 50.3 %shard_map.91 = f32[5,4096]{1,0:T(8,128)} custom-call(bf16[20,8192]{1,0:T(8,128)(2,1)} %x_hbm.1, s32[128]{0:T(128)} %rank_hbm.1, s32[768]{0:T(1024)} %src_hbm.1, s32[768]{0:T(1024)} %dst_hbm.1, s32[1]{0:T(128)S(6)} %copy.11.count_hbm, bf16[768,4096]{1,0:T(8,128)(2,1)} %w_hbm.1, f32[5,4096]{1,0:T(8,128)} %ocean_hbm.1, f32[5]{0:T(128)} %coef_hbm.1, s32[4096]{0:T(1024)} %mask_hbm.1), custom_call_target="tpu_custom_call" | custom-call | tf_op jit(solution)/shard_map/pallas_call | solution.py:409
  50.9 1.6 %copy.12 = f32[5,4096]{1,0:T(8,128)} copy(f32[5,4096]{1,0:T(8,128)} %shard_map.91) | data formatting | bytes 163840
